TPU v7x, 256 devices: a whole 4x4x8 slice. The times are simulated.
256 devices in a mesh: store: 64 (over z, y, core), tp: 4 (over x).
Axes of the slice: x: 4, y: 4, z: 8, core: 2. Of those that a mesh axis runs over, the one named last changes fastest.
Arguments:
- query_embeds: bfloat16 [128, 16, 4096], P('store', None, 'tp'), may hold values from -6 to 6
- passage_embeds: bfloat16 [128, 32, 4096], P('store', None, 'tp'), may hold values from -6 to 6
- passage_lengths: int32 [128], P('store'), may hold values from 1 to 32, as said below
- cand_passage: int32 [1536], P('store'), may hold values from 0 to 127, as said below
- norm_gain: bfloat16 [4096], replicated, may hold values from 0.099609375 to 1.8984375
- w_qkv: bfloat16 [4096, 16, 384], P(None, 'tp'), may hold values from -1 to 1
Outputs:
- query_attn: bfloat16 [128, 16, 2048], P('store', None, 'tp')
- passage_attn: bfloat16 [1536, 32, 2048], P('store', None, 'tp')
Inputs may be any that keep to these rules, and one draw needn't show every extreme that they name: `cand_passage`: passage id p is held by store index p // 2 at position p % 2. Among the 24 pairs of one store index, the passages come from as many different store indices as possible, and no store index holds the passages of more than 1 of them. `passage_lengths`: some passage has 32 tokens.
All inputs are finite; a program needn't handle non-finite values.
Results may differ from a plain program's by a relative error of at most 0.023.
The roundings to bfloat16 on the way count: a program that leaves them out, or rounds other values in their place, can miss the bound.
Values may be sent and summed in bfloat16 or wider, within the bound.
A program may use at most 128 MiB of HBM per device.

v0:
```python
import math

import jax
import jax.numpy as jnp
from jax import lax
from jax.sharding import PartitionSpec as P


def rms_rows(rows, norm_gain):
    values = rows.astype(jnp.float32)
    meansq = jnp.mean(values * values, axis=-1, keepdims=True)
    scaled = values * lax.rsqrt(meansq + 1e-05) * norm_gain.astype(jnp.float32)
    return scaled.astype(jnp.bfloat16)


def rotate_parts(raw, positions, head_dim):
    half_dim = head_dim // 2
    inverse = jnp.exp(
        jnp.arange(half_dim, dtype=jnp.float32) * (-2.0 * math.log(10000.0) / head_dim)
    )
    angles = positions[:, None] * inverse[None, :]
    cosine = jnp.cos(angles)[:, None, :]
    sine_part = jnp.sin(angles)[:, None, :]

    def turned(block):
        first = block[..., :half_dim]
        second = block[..., half_dim:]
        return jnp.concatenate(
            [first * cosine - second * sine_part, second * cosine + first * sine_part], axis=-1
        )

    queries = turned(raw[..., :head_dim])
    keyset = turned(raw[..., head_dim : 2 * head_dim])
    values = raw[..., 2 * head_dim :]
    return jnp.concatenate([queries, keyset, values], axis=-1).astype(jnp.bfloat16)


def softmax_rounded(scores, allowed):
    masked = jnp.where(allowed, scores, jnp.float32(-1e30))
    peak = jnp.max(masked, axis=-1, keepdims=True)
    expon = jnp.where(allowed, jnp.exp(masked - peak), jnp.float32(0.0))
    return (expon / jnp.sum(expon, axis=-1, keepdims=True)).astype(jnp.bfloat16)


def attend_queries(query_qkv, head_dim):
    count, query_len, heads = (query_qkv.shape[0], query_qkv.shape[1], query_qkv.shape[2])
    scale = head_dim ** (-0.5)
    scores = (
        jnp.einsum(
            "bqhd,bkhd->bhqk",
            query_qkv[..., :head_dim],
            query_qkv[..., head_dim : 2 * head_dim],
            preferred_element_type=jnp.float32,
        )
        * scale
    )
    steps_row = jnp.arange(query_len, dtype=jnp.int32)
    allowed = steps_row[:, None] >= steps_row[None, :]
    weights = softmax_rounded(scores, allowed[None, None])
    output = jnp.einsum(
        "bhqk,bkhd->bqhd",
        weights,
        query_qkv[..., 2 * head_dim :],
        preferred_element_type=jnp.float32,
    )
    return output.reshape(count, query_len, heads * head_dim).astype(jnp.bfloat16)


def attend_core(query_kv, pair_qkv, pair_lengths, head_dim):
    query_len = query_kv.shape[1]
    pairs, passage_len, heads = (pair_qkv.shape[0], pair_qkv.shape[1], pair_qkv.shape[2])
    scale = head_dim ** (-0.5)
    keyset = jnp.concatenate(
        [query_kv[..., :head_dim], pair_qkv[..., head_dim : 2 * head_dim]], axis=1
    )
    values = jnp.concatenate([query_kv[..., head_dim:], pair_qkv[..., 2 * head_dim :]], axis=1)
    scores = (
        jnp.einsum(
            "bihd,bthd->bhit", pair_qkv[..., :head_dim], keyset, preferred_element_type=jnp.float32
        )
        * scale
    )
    column = jnp.arange(query_len + passage_len, dtype=jnp.int32) - query_len
    row_index = jnp.arange(passage_len, dtype=jnp.int32)
    allowed = (column[None, None, :] < 0) | (column[None, None, :] <= row_index[None, :, None]) & (
        column[None, None, :] < pair_lengths[:, None, None]
    )
    weights = softmax_rounded(scores, allowed[:, None])
    output = jnp.einsum("bhit,bthd->bihd", weights, values, preferred_element_type=jnp.float32)
    live = row_index[None, :] < pair_lengths[:, None]
    output = jnp.where(live[:, :, None, None], output, jnp.float32(0.0))
    return output.reshape(pairs, passage_len, heads * head_dim).astype(jnp.bfloat16)


def attend_pairs(query_qkv, pair_qkv, pair_lengths, head_dim, cands):
    repeated = jnp.repeat(query_qkv[..., head_dim:], cands, axis=0)
    return attend_core(repeated, pair_qkv, pair_lengths, head_dim)


def local(query_embeds, passage_embeds, passage_lengths, cand_passage, norm_gain, w_qkv):
    n_store = lax.axis_size("store")
    quer_count, query_len, width_part = query_embeds.shape
    pass_count, passage_len = (passage_embeds.shape[0], passage_embeds.shape[1])
    pairs_dev = cand_passage.shape[0]
    cands = pairs_dev // quer_count
    heads_part = w_qkv.shape[1]
    head_dim = w_qkv.shape[2] // 3
    capacity = (pairs_dev + n_store - 1) // n_store
    weights_flat = w_qkv.reshape(w_qkv.shape[0], heads_part * 3 * head_dim)
    query_rows = query_embeds.reshape(quer_count * query_len, width_part)
    query_pos = jnp.tile(jnp.arange(query_len, dtype=jnp.float32), quer_count)
    query_total = quer_count * query_len
    holder = cand_passage // pass_count
    same_holder = holder[:, None] == holder[None, :]
    pair_index = jnp.arange(pairs_dev, dtype=jnp.int32)
    earlier = pair_index[:, None] < pair_index[None, :]
    rank_in = jnp.sum((same_holder & earlier).astype(jnp.int32), axis=0)
    slot_code = cand_passage % pass_count + 1
    hits = (holder[:, None, None] == jnp.arange(n_store, dtype=jnp.int32)[None, :, None]) & (
        rank_in[:, None, None] == jnp.arange(capacity, dtype=jnp.int32)[None, None, :]
    )
    request = jnp.sum(jnp.where(hits, slot_code[:, None, None], 0), axis=0)
    flat_index = holder * capacity + rank_in
    hits, request, flat_index = (hits, request, flat_index)
    incoming = lax.all_to_all(request, "store", split_axis=0, concat_axis=0, tiled=True)
    chosen = jnp.maximum(incoming - 1, 0)
    filled = incoming > 0
    outgoing = jnp.where(
        filled[:, :, None, None], passage_embeds[chosen], jnp.zeros((), passage_embeds.dtype)
    )
    out_len = jnp.where(filled, passage_lengths[chosen], 0)
    arrived = lax.all_to_all(outgoing, "store", split_axis=0, concat_axis=0, tiled=True)
    arrived_len = lax.all_to_all(out_len, "store", split_axis=0, concat_axis=0, tiled=True)
    flat_rows = arrived.reshape((n_store * capacity,) + passage_embeds.shape[1:])
    fetched = flat_rows[flat_index]
    pair_lengths = arrived_len.reshape(n_store * capacity)[flat_index]
    pair_pos = query_len + jnp.tile(jnp.arange(passage_len, dtype=jnp.float32), pairs_dev)
    all_rows = jnp.concatenate(
        [query_rows, fetched.reshape(pairs_dev * passage_len, width_part)], axis=0
    )
    full_rows = lax.all_gather(all_rows, "tp", axis=1, tiled=True)
    normed = rms_rows(full_rows, norm_gain)
    raw = jnp.dot(normed, weights_flat, preferred_element_type=jnp.float32)
    raw = raw.reshape(all_rows.shape[0], heads_part, 3 * head_dim)
    projected = rotate_parts(raw, jnp.concatenate([query_pos, pair_pos], axis=0), head_dim)
    query_qkv = projected[:query_total].reshape(quer_count, query_len, heads_part, 3 * head_dim)
    pair_qkv = projected[query_total:].reshape(pairs_dev, passage_len, heads_part, 3 * head_dim)
    query_attn = attend_queries(query_qkv, head_dim)
    passage_attn = attend_pairs(query_qkv, pair_qkv, pair_lengths, head_dim, cands)
    return (query_attn, passage_attn)


def solution(mesh):
    in_specs = (
        P("store", None, "tp"),
        P("store", None, "tp"),
        P("store"),
        P("store"),
        P(),
        P(None, "tp", None),
    )
    out_specs = (P("store", None, "tp"), P("store", None, "tp"))
    return jax.shard_map(local, mesh=mesh, in_specs=in_specs, out_specs=out_specs, check_vma=False)
```

profile of v0, /device:TPU:1, one launch (start us, length us, event | category | flops | bytes accessed | tf_op | source)
XLA Modules:
  0.0 256.2 jit_solution(16776355402907766415)
XLA Ops:
  8.8 13.2 %all-to-all-start = ((s32[64,1,1]{2,1,0:T(1,128)}), s32[64,1,1]{2,1,0:T(1,128)S(1)}, u32[]{:S(2)}, u32[]{:S(2)}) async-start(s32[64,1,1]{2,1,0:T(1,128)} %copy.58), calls=%async_computation | async-start | bytes 65536 | tf_op jit(solution)/shard_map/all_to_all | solution.py:125
  22.0 1.3 fusion.51
  23.3 8.0 %all-to-all-done = s32[64,1,1]{2,1,0:T(1,128)S(1)} async-done(((s32[64,1,1]{2,1,0:T(1,128)}), s32[64,1,1]{2,1,0:T(1,128)S(1)}, u32[]{:S(2)}, u32[]{:S(2)}) %all-to-all-start) | async-done | bytes 288 | tf_op jit(solution)/shard_map/all_to_all | solution.py:125
  31.3 1.3 compare_select_fusion.5
  32.6 2.8 %gather_fusion = bf16[64,32,1024]{2,1,0:T(8,128)(2,1)} fusion(bf16[2,32,1024]{2,1,0:T(8,128)(2,1)S(1)} %copy-done, s32[1024]{0:T(1024)S(1)} %pad_clamp_fusion.1), kind=kCustom, calls=%fused_computation | custom fusion | bytes 8388864 | tf_op jit(solution)/shard_map/gather | solution.py:129
  35.4 4.5 %bitcast_select_fusion = bf16[64,1,32,1024]{3,2,1,0:T(8,128)(2,1)} fusion(bf16[64,32,1024]{2,1,0:T(8,128)(2,1)} %gather_fusion, pred[64]{0:T(512)(128)(4,1)S(1)} %compare_bitcast_fusion), kind=kLoop, calls=%fused_computation.14 | loop fusion | flops 2097152 | bytes 8388672 | tf_op jit(solution)/shard_map/jit(_where)/select_n | solution.py:128
  39.9 5.7 %all-to-all-start.1 = ((bf16[64,1,32,1024]{3,2,1,0:T(8,128)(2,1)}), bf16[64,1,32,1024]{3,2,1,0:T(8,128)(2,1)}, u32[]{:S(2)}, u32[]{:S(2)}) async-start(bf16[64,1,32,1024]{3,2,1,0:T(8,128)(2,1)} %bitcast_select_fusion), calls=%async_computation.1 | async-start | bytes 8388608 | tf_op jit(solution)/shard_map/all_to_all | solution.py:132
  45.7 94.6 %all-to-all-done.1 = bf16[64,1,32,1024]{3,2,1,0:T(8,128)(2,1)} async-done(((bf16[64,1,32,1024]{3,2,1,0:T(8,128)(2,1)}), bf16[64,1,32,1024]{3,2,1,0:T(8,128)(2,1)}, u32[]{:S(2)}, u32[]{:S(2)}) %all-to-all-start.1) | async-done | bytes 4194336 | tf_op jit(solution)/shard_map/all_to_all | solution.py:132
  140.3 2.8 %gather_fusion.1 = bf16[24,32,1024]{2,1,0:T(8,128)(2,1)S(1)} fusion(bf16[64,32,1024]{2,1,0:T(8,128)(2,1)} %bitcast.5, s32[1024]{0:T(1024)S(1)} %pad_clamp_fusion), kind=kCustom, calls=%fused_computation.1 | custom fusion | bytes 3145824 | tf_op jit(solution)/shard_map/gather | solution.py:135
  143.1 1.3 pad_maximum_fusion
  144.7 1.5 multiply_cosine_fusion
  147.0 7.0 %all-to-all-start.2 = ((s32[64,1,1]{2,1,0:T(1,128)}), s32[64,1,1]{2,1,0:T(1,128)S(1)}, u32[]{:S(2)}, u32[]{:S(2)}) async-start(s32[64,1,1]{2,1,0:T(1,128)} %copy.67), calls=%async_computation.2 | async-start | bytes 65536 | tf_op jit(solution)/shard_map/all_to_all | solution.py:133
  154.0 12.9 %copy.82 = bf16[512,8,4,384]{3,1,2,0:T(8,128)(2,1)} copy(bf16[512,8,4,384]{3,2,1,0:T(4,128)(2,1)} %bitcast.43) | data formatting | bytes 25165824
  166.9 16.7 %copy.61 = bf16[1536,4096]{1,0:T(8,128)(2,1)} copy(bf16[1536,4096]{0,1:T(8,128)(2,1)} %bitcast.42) | data formatting | bytes 25165824 | tf_op jit(solution)/shard_map/dot_general | solution.py:143
  183.6 1.2 reduce.1
  185.8 26.8 %all-gather.2.cloned.1.call-done = bf16[800,4096]{1,0:T(8,128)(2,1)} async-done(((bf16[800,1024]{1,0:T(8,128)(2,1)}), bf16[800,4096]{1,0:T(8,128)(2,1)}) %all-gather.2.cloned.1.call-update) | async-done | bytes 6553616 | tf_op jit(solution)/shard_map/all_gather | solution.py:141
  212.6 4.4 %fusion.2 = f32[800]{0:T(1024)S(1)} fusion(bf16[800,4096]{1,0:T(8,128)(2,1)} %all-gather.2.cloned.1.call-done), kind=kLoop, calls=%fused_computation.7 | loop fusion | flops 9829600 | bytes 6556800 | tf_op jit(solution)/shard_map/reduce_sum | solution.py:11
  217.4 13.5 %fusion.6 = f32[800,4,384]{2,0,1:T(8,128)S(1)} fusion(bf16[4,384,4096]{2,1,0:T(8,128)(2,1)} %bitcast.44, bf16[800,4096]{1,0:T(8,128)(2,1)S(1)} %copy-done.3, f32[4096]{0:T(1024)S(1)} %convert_element_type.39, f32[800]{0:T(1024)S(1)} %add_rsqrt_fusion), kind=kOutput, calls=%fused_computation.11 | convolution fusion | flops 10079436800 | bytes 24071296 | tf_op jit(solution)/shard_map/dot_general | solution.py:143
  230.9 2.7 %add_convert_fusion = (bf16[800,4,64]{2,0,1:T(8,128)(2,1)}, bf16[800,4,64]{2,0,1:T(8,128)(2,1)}, bf16[800,4,64]{2,0,1:T(8,128)(2,1)}, bf16[800,4,64]{2,0,1:T(8,128)(2,1)}) fusion(f32[800,4,384]{2,0,1:T(8,128)S(1)} %fusion.6, f32[800,64]{1,0:T(8,128)S(1)} %get-tuple-element.15, f32[800,64]{1,0:T(8,128)S(1)} %get-tuple-element.14), kind=kLoop, calls=%fused_computation.18 | loop fusion | flops 3276800 | bytes 5324800 | tf_op jit(solution)/shard_map/convert.3
  233.7 5.8 %concatenate.18 = bf16[800,4,384]{2,0,1:T(8,128)(2,1)S(1)} concatenate(bf16[800,4,64]{2,0,1:T(8,128)(2,1)} %get-tuple-element.4, bf16[800,4,64]{2,0,1:T(8,128)(2,1)} %get-tuple-element.5, bf16[800,4,64]{2,0,1:T(8,128)(2,1)} %get-tuple-element.3, bf16[800,4,64]{2,0,1:T(8,128)(2,1)} %get-tuple-element.2, bf16[800,4,128]{2,0,1:T(8,128)(2,1)S(1)} %slice.105), dimensions={2} | concatenate | bytes 4915200 | tf_op jit(solution)/shard_map/concatenate | solution.py:35
  239.6 1.4 copy-done.2
  242.1 1.1 fusion.49
  243.2 1.7 fusion.48
  244.9 2.6 %fusion.53 = (f32[24,4,32]{2,1,0:T(4,128)S(1)}, f32[24,4,32,48]{3,2,1,0:T(8,128)S(1)}) fusion(bf16[24,16,4,128]{3,1,2,0:T(8,128)(2,1)} %get-tuple-element.9, bf16[24,32,4,128]{3,1,0,2:T(8,128)(2,1)} %get-tuple-element.6, pred[24,32,48]{2,1,0:T(8,128)(4,1)S(1)} %and_or_fusion, bf16[24,32,4,128]{3,1,0,2:T(8,128)(2,1)} %get-tuple-element.7), kind=kOutput, calls=%fused_computation.94 | convolution fusion | flops 40845360 | bytes 2605056 | tf_op jit(solution)/shard_map/sub | solution.py:41
  (56 shorter events, 7.2 us)
Async XLA Ops:
  7.2 25.5 %copy-start = (bf16[2,32,1024]{2,1,0:T(8,128)(2,1)S(1)}, bf16[2,32,1024]{2,1,0:T(8,128)(2,1)}, u32[]{:S(2)}) copy-start(bf16[2,32,1024]{2,1,0:T(8,128)(2,1)} %param.7) | copy-start | bytes 393220
  8.8 22.5 %all-to-all-start = ((s32[64,1,1]{2,1,0:T(1,128)}), s32[64,1,1]{2,1,0:T(1,128)S(1)}, u32[]{:S(2)}, u32[]{:S(2)}) async-start(s32[64,1,1]{2,1,0:T(1,128)} %copy.58), calls=%async_computation | async-start | bytes 65536 | tf_op jit(solution)/shard_map/all_to_all | solution.py:125
  39.9 100.4 %all-to-all-start.1 = ((bf16[64,1,32,1024]{3,2,1,0:T(8,128)(2,1)}), bf16[64,1,32,1024]{3,2,1,0:T(8,128)(2,1)}, u32[]{:S(2)}, u32[]{:S(2)}) async-start(bf16[64,1,32,1024]{3,2,1,0:T(8,128)(2,1)} %bitcast_select_fusion), calls=%async_computation.1 | async-start | bytes 8388608 | tf_op jit(solution)/shard_map/all_to_all | solution.py:132
  45.6 97.5 %copy-start.5 = (bf16[2,16,1024]{2,1,0:T(8,128)(2,1)S(1)}, bf16[2,16,1024]{2,1,0:T(8,128)(2,1)}, u32[]{:S(2)}) copy-start(bf16[2,16,1024]{2,1,0:T(8,128)(2,1)} %param.6) | copy-start | bytes 196612
  45.6 167.0 %all-gather.2.cloned.1.call-start = ((), (), s32[]{:S(2)}) async-start(), calls=%async_computation.3 | async-start | bytes 8192000 | tf_op jit(solution)/shard_map/all_gather | solution.py:141
  147.0 36.7 %all-to-all-start.2 = ((s32[64,1,1]{2,1,0:T(1,128)}), s32[64,1,1]{2,1,0:T(1,128)S(1)}, u32[]{:S(2)}, u32[]{:S(2)}) async-start(s32[64,1,1]{2,1,0:T(1,128)} %copy.67), calls=%async_computation.2 | async-start | bytes 65536 | tf_op jit(solution)/shard_map/all_to_all | solution.py:133
  166.9 16.7 %copy-start.6 = (bf16[4096]{0:T(1024)(128)(2,1)S(1)}, bf16[4096]{0:T(1024)(128)(2,1)}, u32[]{:S(2)}) copy-start(bf16[4096]{0:T(1024)(128)(2,1)} %param.10) | copy-start | bytes 24580
  212.6 4.7 %copy-start.3 = (bf16[800,4096]{1,0:T(8,128)(2,1)S(1)}, bf16[800,4096]{1,0:T(8,128)(2,1)}, u32[]{:S(2)}) copy-start(bf16[800,4096]{1,0:T(8,128)(2,1)} %all-gather.2.cloned.1.call-done) | copy-start | bytes 19660804
  239.5 1.4 copy-start.2
  240.9 2.2 slice-start
  244.9 2.6 %copy-start.4 = (bf16[24,16,4,128]{3,1,2,0:T(8,128)(2,1)S(1)}, bf16[24,16,4,128]{3,1,2,0:T(8,128)(2,1)}, u32[]{:S(2)}) copy-start(bf16[24,16,4,128]{3,1,2,0:T(8,128)(2,1)} %get-tuple-element.10) | copy-start | bytes 1179652
  247.5 1.9 copy-start.1
Sparse Core Ops, SparseCore 0:
  144.6 67.9 all-gather.1
where the time goes:
time: 257 us; the launch traced here: 256 us
  waiting for transfers between devices  129 us (50%)
  local copies, waits for them, and re-layouts  51.2 us (20%)
  starting transfers between devices  25.9 us (10%)
  other arithmetic  18.1 us (7%)
  matrix products  17.3 us (7%)
  between operations  14.3 us (6%)
    all_to_all x1, waiting for transfers between devices, local(): lax.all_to_all(outgoing, 'store', split_axis=0, concat_axis=0, tiled=True)  94.6 us
    all_gather x1, waiting for transfers between devices, local(): full_rows = lax.all_gather(all_rows, 'tp', axis=1, tiled=True)  26.8 us
    dot_general x1, local copies, waits for them, and re-layouts, local(): raw = jnp.dot(normed, weights_flat, preferred_element_type=jnp.float32)  16.7 us
    unnamed x15, local copies, waits for them, and re-layouts  14.7 us
    dot_general x1, matrix products, local(): raw = jnp.dot(normed, weights_flat, preferred_element_type=jnp.float32)  13.5 us
    all_to_all x1, starting transfers between devices, local(): lax.all_to_all(request, 'store', split_axis=0, concat_axis=0, tiled=True)  13.2 us
    all_to_all x1, waiting for transfers between devices, local(): lax.all_to_all(request, 'store', split_axis=0, concat_axis=0, tiled=True)  7.98 us
    all_to_all x1, starting transfers between devices, local(): lax.all_to_all(out_len, 'store', split_axis=0, concat_axis=0, tiled=True)  7.01 us
  transfers between devices with their start and end apart: 4, of which 3 were waited for; matrix products, arithmetic and copies ran while one was open for 14% of the time, Pallas kernels for 0%

commit v1 on v0

v1 whole, which is shorter than its diff:
```python
import functools
import math

import jax
import jax.numpy as jnp
import numpy as np
from jax import lax
from jax.experimental import pallas as pl
from jax.experimental.pallas import tpu as pltpu
from jax.sharding import PartitionSpec as P

MESH = pl.DeviceIdType.MESH
NZ, NY = 8, 4
D, DPART, HEADS, HD = 4096, 1024, 4, 128
QLEN, PLEN, CANDS, PAIRS = 16, 32, 12, 24
PROWS, QROWS = 2 * PLEN, 2 * QLEN
A_TILES = 5 * 4 + 1
B_TILES = 3 * 4 + 1
A_AT = {"q0": 0, "o0": 1, "q1": 2, "o1": 3, "q2": 4}
B_AT = {"o2": 0, "q3": 1, "o3": 2}
DEAD = 1e30
W_CUTS = 8
Z_GROUPS = ((0, 1), (1, 2), (3, 2), (5, 2), (7, 1))
Y_GROUPS = ((0, 1), (1, 2), (3, 1))
N_SEMS = 160


def tables():
    inverse = np.exp(np.arange(64, dtype=np.float32) * np.float32(-2.0 * math.log(10000.0) / HD))
    where = np.concatenate([np.tile(QLEN + np.arange(PLEN), 2), np.tile(np.arange(QLEN), 2)])
    angles = (where.astype(np.float32)[:, None] * inverse[None, :].astype(np.float32)).astype(np.float64)
    cosine, sine = np.cos(angles), np.sin(angles)
    return np.stack(
        [np.concatenate([cosine, cosine], 1), np.concatenate([-sine, sine], 1)]
    ).astype(np.float32)


def dot_nt(a, b):
    return lax.dot_general(a, b, (((1,), (1,)), ((), ())), preferred_element_type=jnp.float32)


def dot_tn(a, b):
    return lax.dot_general(a, b, (((0,), (0,)), ((), ())), preferred_element_type=jnp.float32)


def kernel(
    len_ref, cand_ref, q_ref, p_ref, gain_ref, table_ref, w_ref, qo_ref, po_ref,
    px, qx, wv, wr, acc, gain_wide, ga, gb, got_q, got_o, stats, qk, qv, w_sem, send, recv,
):
    store, me_x = lax.axis_index("store"), lax.axis_index("tp")
    z, y, core = lax.div(store, 8), lax.rem(lax.div(store, 2), 4), lax.rem(store, 2)
    scale = HD ** (-0.5)

    def at(zz, yy, cc, xx):
        return {"store": (lax.rem(zz, NZ) * NY + lax.rem(yy, NY)) * 2 + cc, "tp": lax.rem(xx, 4)}

    z_up, z_down = at(z + 1, y, core, me_x), at(z + NZ - 1, y, core, me_x)
    y_up, y_down = at(z, y + 1, core, me_x), at(z, y + NY - 1, core, me_x)
    x_up, x_down = at(z, y, core, me_x + 1), at(z, y, core, me_x + 3)
    sibling = at(z, y, 1 - core, me_x)
    even = core == 0
    z_last = at(jnp.where(even, z + 1, z + NZ - 1), y, core, me_x)
    y_last = at(z, jnp.where(even, y + 1, y + NY - 1), core, me_x)

    made = []

    def copy(src, dst, device):
        k = len(made)
        c = pltpu.make_async_remote_copy(
            src, dst, send.at[k], recv.at[k], device_id=device, device_id_type=MESH
        )
        made.append(c)
        c.start()
        return c

    cut = D // W_CUTS
    w_copies = [
        pltpu.make_async_copy(w_ref.at[pl.ds(i * cut, cut)], wv.at[pl.ds(i * cut, cut)], w_sem.at[i])
        for i in range(W_CUTS)
    ]
    for c in w_copies:
        c.start()

    barrier = pltpu.get_barrier_semaphore()
    near = (z_up, z_down, y_up, y_down, x_up, x_down, sibling)
    for device in near:
        pl.semaphore_signal(barrier, inc=1, device_id=device, device_id_type=MESH)
    pl.semaphore_wait(barrier, len(near))

    left, right = lax.rem(me_x + 3, 4), lax.rem(me_x + 1, 4)
    p_hop = [copy(p_ref, px.at[me_x], x_up), copy(p_ref, px.at[me_x], x_down)]
    q_hop = [copy(q_ref, qx.at[me_x], x_up), copy(q_ref, qx.at[me_x], x_down)]
    for c in range(4):
        gain_wide[c] = gain_ref[pl.ds(c * DPART, DPART)].astype(jnp.float32).reshape(1, DPART)
    px[me_x] = p_ref[...]
    qx[me_x] = q_ref[...]

    for i, c in enumerate(w_copies):
        c.wait()

        @pl.loop(0, cut // 64)
        def _(j):
            row = pl.multiple_of(i * cut + j * 64, 64)
            for h in range(HEADS):
                wr[pl.ds(row, 64), h * 384 : (h + 1) * 384] = wv[pl.ds(row, 64), h, :]

    for c in p_hop:
        c.wait_recv()
    low, high = pl.ds(0, PLEN), pl.ds(PLEN, PLEN)
    p_far = [
        copy(px.at[left, low], px.at[left, low], x_up),
        copy(px.at[right, high], px.at[right, high], x_down),
    ]
    for c in q_hop:
        c.wait_recv()
    low, high = pl.ds(0, QLEN), pl.ds(QLEN, QLEN)
    q_far = [
        copy(qx.at[left, low], qx.at[left, low], x_up),
        copy(qx.at[right, high], qx.at[right, high], x_down),
    ]

    def project(rows_ref, rows):
        total = jnp.zeros((rows, 1), jnp.float32)
        for c in range(4):
            values = rows_ref[c].astype(jnp.float32)
            total = total + jnp.sum(values * values, axis=-1, keepdims=True)
        inverse = lax.rsqrt(total * (1.0 / D) + 1e-05)
        acc[pl.ds(0, rows), :] = jnp.zeros((rows, HEADS * 384), jnp.float32)

        @pl.loop(0, 4)
        def _(c):
            values = rows_ref[c].astype(jnp.float32)
            gain = gain_wide[c]
            normed = (values * inverse * gain).astype(jnp.bfloat16)
            depth = pl.ds(pl.multiple_of(c * DPART, DPART), DPART)
            acc[pl.ds(0, rows), :] += jnp.dot(
                normed, wr[depth, :], preferred_element_type=jnp.float32
            )

    def turned(part, rows, row0):
        cosine, sine = table_ref[0, pl.ds(row0, rows), :], table_ref[1, pl.ds(row0, rows), :]
        return (part * cosine + pltpu.roll(part, 64, 1) * sine).astype(jnp.bfloat16)

    for c in p_far:
        c.wait_recv()
    project(px, PROWS)

    row = lax.broadcasted_iota(jnp.int32, (PROWS, PROWS), 0)
    col = lax.broadcasted_iota(jnp.int32, (PROWS, PROWS), 1)
    seen = (col <= row) & (lax.div(row, PLEN) == lax.div(col, PLEN))
    out_row = lax.broadcasted_iota(jnp.int32, (PROWS, HD), 0)
    len0, len1 = len_ref[0], len_ref[1]
    live = lax.rem(out_row, PLEN) < jnp.where(out_row < PLEN, len0, len1)
    key_row = lax.broadcasted_iota(jnp.int32, (PLEN, 128), 0)
    token = lax.rem(lax.broadcasted_iota(jnp.int32, (PLEN, 128), 1), PLEN)
    seen_t = key_row <= token
    token_row = lax.rem(lax.broadcasted_iota(jnp.int32, (1, 128), 1), PLEN)
    stat_row = lax.broadcasted_iota(jnp.int32, (16, 128), 0)
    stat = [jnp.zeros((16, 128), jnp.float32), jnp.zeros((16, 128), jnp.float32)]

    def put(name, value):
        where, slots = (ga, A_AT) if name in A_AT else (gb, B_AT)
        where[0, pl.ds(slots[name] * 4, 4)] = value.reshape(4, 16, HD)

    for h in range(HEADS):
        queries = turned(acc[pl.ds(0, PROWS), h * 384 : h * 384 + 128], PROWS, 0)
        keys = turned(acc[pl.ds(0, PROWS), h * 384 + 128 : h * 384 + 256], PROWS, 0)
        values = acc[pl.ds(0, PROWS), h * 384 + 256 : h * 384 + 384].astype(jnp.bfloat16)
        scores = jnp.where(seen, dot_nt(queries, keys) * scale, -1e30)
        peak = jnp.max(scores, axis=-1, keepdims=True)
        expon = jnp.where(seen, jnp.exp(scores - peak), 0.0)
        weights = (expon / jnp.sum(expon, axis=-1, keepdims=True)).astype(jnp.bfloat16)
        own = jnp.dot(weights, values, preferred_element_type=jnp.float32)
        put(f"q{h}", queries)
        put(f"o{h}", jnp.where(live, own, 0.0).astype(jnp.bfloat16))
        for j in range(2):
            some = queries[j * PLEN : (j + 1) * PLEN]
            turned_scores = dot_nt(
                keys[j * PLEN : (j + 1) * PLEN], jnp.concatenate([some] * 4, axis=0)
            )
            turned_scores = jnp.where(seen_t, turned_scores * scale, -1e30)
            top = jnp.max(turned_scores, axis=0, keepdims=True)
            mass = jnp.sum(jnp.where(seen_t, jnp.exp(turned_scores - top), 0.0), axis=0, keepdims=True)
            level = jnp.where(token_row < (len0, len1)[j], top + jnp.log(mass), DEAD)
            coarse = level.astype(jnp.bfloat16).astype(jnp.float32)
            at_row = j * 8 + 2 * (h % 2)
            block = stat[h // 2]
            block = jnp.where(stat_row == at_row, coarse, block)
            stat[h // 2] = jnp.where(stat_row == at_row + 1, level - coarse, block)
    ga[0, A_TILES - 1] = stat[0].astype(jnp.bfloat16)
    gb[0, B_TILES - 1] = stat[1].astype(jnp.bfloat16)

    def a_slots(half, ys, zs, n):
        return ga.at[pl.ds(half * 32 + ys * 8 + zs, n)]

    def b_slots(half, zs, ys, n):
        return gb.at[pl.ds(half * 32 + zs * 4 + ys, n)]

    def a_z(step):
        if step == 3:
            return [copy(a_slots(0, 0, jnp.where(even, 6, 5), 1), a_slots(0, 0, 7, 1), z_last)]
        up, down = (0, 2, 4)[step], (0, 1, 3)[step]
        return [
            copy(a_slots(0, 0, up, 1), a_slots(0, 0, 2 * step + 2, 1), z_up),
            copy(a_slots(0, 0, down, 1), a_slots(0, 0, 2 * step + 1, 1), z_down),
        ]

    def a_y(g):
        zs, n = Z_GROUPS[g]
        return [
            copy(a_slots(0, 0, zs, n), a_slots(0, 2, zs, n), y_up),
            copy(a_slots(0, 0, zs, n), a_slots(0, 1, zs, n), y_down),
        ]

    def a_y_last(g):
        zs, n = Z_GROUPS[g]
        return [copy(a_slots(0, jnp.where(even, 2, 1), zs, n), a_slots(0, 3, zs, n), y_last)]

    def a_sib(ys, g):
        zs, n = Z_GROUPS[g]
        return copy(a_slots(0, ys, zs, n), a_slots(1, ys, zs, n), sibling)

    def b_y():
        return [
            copy(b_slots(0, 0, 0, 1), b_slots(0, 0, 2, 1), y_up),
            copy(b_slots(0, 0, 0, 1), b_slots(0, 0, 1, 1), y_down),
        ]

    def b_y_last():
        return [copy(b_slots(0, 0, jnp.where(even, 2, 1), 1), b_slots(0, 0, 3, 1), y_last)]

    def b_z(e, step):
        ys, n = Y_GROUPS[e]
        if step == 3:
            return [copy(b_slots(0, jnp.where(even, 6, 5), ys, n), b_slots(0, 7, ys, n), z_last)]
        up, down = (0, 2, 4)[step], (0, 1, 3)[step]
        return [
            copy(b_slots(0, up, ys, n), b_slots(0, 2 * step + 2, ys, n), z_up),
            copy(b_slots(0, down, ys, n), b_slots(0, 2 * step + 1, ys, n), z_down),
        ]

    def b_sib(g):
        zs, n = Z_GROUPS[g]
        return copy(b_slots(0, zs, 0, 4 * n), b_slots(1, zs, 0, 4 * n), sibling)

    def arrived(copies):
        for c in copies:
            c.wait_recv()

    a_sibs, b_sibs = [], []
    az = {0: a_z(0)}
    ay = {0: a_y(0)}
    by = b_y()
    bz = {(0, 0): b_z(0, 0)}
    a_sibs.append(a_sib(0, 0))

    for c in q_far:
        c.wait_recv()
    project(qx, QROWS)

    arrived(az[0])
    az[1], ay[1] = a_z(1), a_y(1)
    arrived(ay[0])
    ayl = {0: a_y_last(0)}
    arrived(by)
    byl = b_y_last()
    bz[1, 0] = b_z(1, 0)
    arrived(bz[0, 0])
    bz[0, 1] = b_z(0, 1)
    a_sibs += [a_sib(0, 1), a_sib(1, 0), a_sib(2, 0)]

    q_at = lax.broadcasted_iota(jnp.int32, (QROWS, QROWS), 0)
    k_at = lax.broadcasted_iota(jnp.int32, (QROWS, QROWS), 1)
    q_seen = (k_at <= q_at) & (lax.div(q_at, QLEN) == lax.div(k_at, QLEN))
    for h in range(HEADS):
        queries = turned(acc[pl.ds(0, QROWS), h * 384 : h * 384 + 128], QROWS, PROWS)
        keys = turned(acc[pl.ds(0, QROWS), h * 384 + 128 : h * 384 + 256], QROWS, PROWS)
        values = acc[pl.ds(0, QROWS), h * 384 + 256 : h * 384 + 384].astype(jnp.bfloat16)
        qk[h], qv[h] = keys, values
        scores = jnp.where(q_seen, dot_nt(queries, keys) * scale, -1e30)
        peak = jnp.max(scores, axis=-1, keepdims=True)
        expon = jnp.where(q_seen, jnp.exp(scores - peak), 0.0)
        weights = (expon / jnp.sum(expon, axis=-1, keepdims=True)).astype(jnp.bfloat16)
        own = jnp.dot(weights, values, preferred_element_type=jnp.float32)
        qo_ref[:, h * HD : (h + 1) * HD] = own.astype(jnp.bfloat16)

    arrived(az[1])
    az[2], ay[2] = a_z(2), a_y(2)
    arrived(ay[1])
    ayl[1] = a_y_last(1)
    arrived(byl)
    bz[2, 0] = b_z(2, 0)
    arrived(bz[1, 0])
    bz[1, 1] = b_z(1, 1)
    arrived(bz[0, 1])
    bz[0, 2] = b_z(0, 2)
    arrived(ayl[0])
    b_sibs.append(b_sib(0))
    a_sibs += [a_sib(0, 2), a_sib(1, 1), a_sib(2, 1), a_sib(3, 0)]

    arrived(az[2])
    az[3], ay[3] = a_z(3), a_y(3)
    arrived(ay[2])
    ayl[2] = a_y_last(2)
    arrived(bz[2, 0])
    bz[2, 1] = b_z(2, 1)
    arrived(bz[1, 1])
    bz[1, 2] = b_z(1, 2)
    arrived(bz[0, 2])
    bz[0, 3] = b_z(0, 3)
    arrived(ayl[1])
    b_sibs.append(b_sib(1))
    a_sibs += [a_sib(0, 3), a_sib(1, 2), a_sib(2, 2), a_sib(3, 1)]

    arrived(az[3])
    ay[4] = a_y(4)
    arrived(ay[3])
    ayl[3] = a_y_last(3)
    arrived(bz[2, 1])
    bz[2, 2] = b_z(2, 2)
    arrived(bz[1, 2])
    bz[1, 3] = b_z(1, 3)
    arrived(ayl[2])
    b_sibs.append(b_sib(2))
    a_sibs += [a_sib(0, 4), a_sib(1, 3), a_sib(2, 3), a_sib(3, 2)]

    arrived(ay[4])
    ayl[4] = a_y_last(4)
    arrived(bz[2, 2])
    bz[2, 3] = b_z(2, 3)
    arrived(bz[0, 3])
    arrived(bz[1, 3])
    arrived(ayl[3])
    b_sibs.append(b_sib(3))
    a_sibs += [a_sib(1, 4), a_sib(2, 4), a_sib(3, 3)]

    arrived(ayl[4])
    a_sibs.append(a_sib(3, 4))
    arrived(bz[2, 3])
    b_sibs.append(b_sib(4))

    lane = lax.div(lax.broadcasted_iota(jnp.int32, (8, 128), 1), PLEN)
    first_row = lax.broadcasted_iota(jnp.int32, (QLEN, CANDS * PLEN), 0)
    ones = jnp.where(
        lax.broadcasted_iota(jnp.int32, (QLEN, HD), 0) < 2, 1.0, 0.0
    ).astype(jnp.bfloat16)

    def place(m):
        passage = cand_ref[m]
        holder = lax.div(passage, 2)
        dz = lax.rem(lax.div(holder, 8) - z + NZ, NZ)
        dy = lax.rem(lax.rem(lax.div(holder, 2), NY) - y + NY, NY)
        zs = dz * 2 - 1 + lax.div(7 - dz, 7) + lax.div(dz, 5) * (17 - 4 * dz)
        ys = dy * 2 - 1 + lax.div(3 - dy, 3) + lax.div(dy, 3) * (9 - 4 * dy)
        other = lax.rem(holder, 2) - core
        return other * other, ys, zs, lax.rem(passage, 2)

    def fetch(where, slots, from_place, part, stat_at):
        @pl.loop(0, PAIRS)
        def _(m):
            half, ys, zs, pos = place(m)
            slot = from_place(half, ys, zs)
            to = pl.ds(pl.multiple_of(m * PLEN, PLEN), PLEN)
            for name, unit in slots.items():
                block = where[slot, pl.ds(unit * 4 + pos * 2, 2)].reshape(PLEN, HD)
                into = got_q if name[0] == "q" else got_o
                into[int(name[1]), to, :] = block
            both = where[slot, stat_at].astype(jnp.float32)
            second = pos.astype(jnp.float32)
            stats[part, m] = both[:8] * (1.0 - second) + both[8:] * second

    def attend(part):
        for q in range(2):
            thirds = []
            for v in range(3):
                block = stats[part, q * CANDS + 4 * v]
                for j in range(1, 4):
                    block = jnp.where(lane == j, stats[part, q * CANDS + 4 * v + j], block)
                thirds.append(block)
            levels = jnp.concatenate(thirds, axis=1)
            rows = pl.ds(q * CANDS * PLEN, CANDS * PLEN)
            for i in range(2):
                h = 2 * part + i
                level = levels[2 * i : 2 * i + 1] + levels[2 * i + 1 : 2 * i + 2]
                scores = dot_nt(qk[h, pl.ds(q * QLEN, QLEN), :], got_q[h, rows, :]) * scale
                peak = jnp.maximum(jnp.max(scores, axis=0, keepdims=True), level)
                expon = jnp.exp(scores - peak)
                rest = jnp.exp(level - peak)
                whole = jnp.sum(expon, axis=0, keepdims=True) + rest
                weights = (expon / whole).astype(jnp.bfloat16)
                share = rest / whole
                coarse = share.astype(jnp.bfloat16).astype(jnp.float32)
                share = jnp.where(
                    first_row == 0, coarse, jnp.where(first_row == 1, share - coarse, 0.0)
                ).astype(jnp.bfloat16)
                out = dot_tn(weights, qv[h, pl.ds(q * QLEN, QLEN), :])
                out = out + dot_tn(share, ones) * got_o[h, rows, :].astype(jnp.float32)
                po_ref[rows, h * HD : (h + 1) * HD] = out.astype(jnp.bfloat16)

    arrived(a_sibs)
    fetch(ga, A_AT, lambda half, ys, zs: half * 32 + ys * 8 + zs, 0, A_TILES - 1)
    attend(0)
    arrived(b_sibs)
    fetch(gb, B_AT, lambda half, ys, zs: half * 32 + zs * 4 + ys, 1, B_TILES - 1)
    attend(1)

    for c in made:
        c.wait_send()


def local(query_embeds, passage_embeds, passage_lengths, cand_passage, norm_gain, w_qkv):
    bf16, f32 = jnp.bfloat16, jnp.float32
    vmem = pl.BlockSpec(memory_space=pltpu.VMEM)
    smem = pl.BlockSpec(memory_space=pltpu.SMEM)
    query_attn, passage_attn = pl.pallas_call(
        kernel,
        out_shape=(
            jax.ShapeDtypeStruct((QROWS, HEADS * HD), bf16),
            jax.ShapeDtypeStruct((PAIRS * PLEN, HEADS * HD), bf16),
        ),
        in_specs=[smem, smem, vmem, vmem, vmem, vmem, pl.BlockSpec(memory_space=pl.ANY)],
        out_specs=(vmem, vmem),
        scratch_shapes=[
            pltpu.VMEM((4, PROWS, DPART), bf16),
            pltpu.VMEM((4, QROWS, DPART), bf16),
            pltpu.VMEM((D, HEADS, 384), bf16),
            pltpu.VMEM((D, HEADS * 384), bf16),
            pltpu.VMEM((PROWS, HEADS * 384), f32),
            pltpu.VMEM((4, 1, DPART), f32),
            pltpu.VMEM((64, A_TILES, 16, HD), bf16),
            pltpu.VMEM((64, B_TILES, 16, HD), bf16),
            pltpu.VMEM((HEADS, PAIRS * PLEN, HD), bf16),
            pltpu.VMEM((HEADS, PAIRS * PLEN, HD), bf16),
            pltpu.VMEM((2, PAIRS, 8, 128), f32),
            pltpu.VMEM((HEADS, QROWS, HD), bf16),
            pltpu.VMEM((HEADS, QROWS, HD), bf16),
            pltpu.SemaphoreType.DMA((W_CUTS,)),
            pltpu.SemaphoreType.DMA((N_SEMS,)),
            pltpu.SemaphoreType.DMA((N_SEMS,)),
        ],
        compiler_params=pltpu.CompilerParams(
            collective_id=0, has_side_effects=True, vmem_limit_bytes=56 * 2**20
        ),
    )(
        passage_lengths,
        cand_passage,
        query_embeds.reshape(QROWS, DPART),
        passage_embeds.reshape(PROWS, DPART),
        norm_gain,
        jnp.asarray(tables()),
        w_qkv,
    )
    return (
        query_attn.reshape(2, QLEN, HEADS * HD),
        passage_attn.reshape(PAIRS, PLEN, HEADS * HD),
    )


def solution(mesh):
    in_specs = (
        P("store", None, "tp"),
        P("store", None, "tp"),
        P("store"),
        P("store"),
        P(),
        P(None, "tp", None),
    )
    out_specs = (P("store", None, "tp"), P("store", None, "tp"))
    return jax.shard_map(local, mesh=mesh, in_specs=in_specs, out_specs=out_specs, check_vma=False)
```

time: 257 us -> 87.7 us (0.34)
  waiting for transfers between devices: 129 us -> 0 us
  Pallas kernels: 0 us -> 83.4 us
  local copies, waits for them, and re-layouts: 51.2 us -> 3.46 us
  starting transfers between devices: 25.9 us -> 0 us
  other arithmetic: 18.1 us -> 0 us
  matrix products: 17.3 us -> 0 us
  between operations: 14.3 us -> 0.64 us
    all_to_all x3 -> x0, waiting for transfers between devices: 103 us -> none  [the longest x1 94.6 us: local(): lax.all_to_all(outgoing, 'store', split_axis=0, concat_axis=0, tiled=True)]
    pallas_call x0 -> x1, Pallas kernels: none -> 83.4 us  [local(): pl.pallas_call(kernel, out_shape=(jax.ShapeDtypeStruct((QROWS, HEADS * HD...]
    all_gather x1 -> x0, waiting for transfers between devices: 26.8 us -> none  [local(): full_rows = lax.all_gather(all_rows, 'tp', axis=1, tiled=True)]
    all_to_all x3 -> x0, starting transfers between devices: 25.9 us -> none  [the longest x1 13.2 us: local(): lax.all_to_all(request, 'store', split_axis=0, concat_axis=0, tiled=True)]
    dot_general x1 -> x0, local copies, waits for them, and re-layouts: 16.7 us -> none  [local(): raw = jnp.dot(normed, weights_flat, preferred_element_type=jnp.float32)]
    dot_general x3 -> x0, matrix products: 14.5 us -> none  [the longest x1 13.5 us: local(): raw = jnp.dot(normed, weights_flat, preferred_element_type=jnp.float32)]
    unnamed x15 -> x2, local copies, waits for them, and re-layouts: 14.7 us -> 3.46 us
    gather x4 -> x0, local copies, waits for them, and re-layouts: 7.64 us -> none  [the longest x1 2.83 us: local(): fetched = flat_rows[flat_index]]
  transfers between devices with their start and end apart: 4 -> 0, of which waited for: 3 -> 0; matrix products, arithmetic and copies ran while one was open for 14% -> 0% of each run, Pallas kernels for 0% -> 0%
where the time goes in v1:
time: 87.7 us; the launch traced here: 87.5 us
  Pallas kernels  83.4 us (95%)
  local copies, waits for them, and re-layouts  3.46 us (4%)
    pallas_call x1, Pallas kernels, local(): pl.pallas_call(kernel, out_shape=(jax.ShapeDtypeStruct((QROWS, HEADS * HD...  83.4 us
    unnamed x2, local copies, waits for them, and re-layouts  3.46 us

profile of v1, /device:TPU:1, one launch (start us, length us, event | category | flops | bytes accessed | tf_op | source)
XLA Modules:
  0.0 87.5 jit_solution(4908887587816340296)
XLA Ops:
  0.6 83.4 %shard_map.86 = (bf16[32,512]{1,0:T(8,128)(2,1)}, bf16[768,512]{1,0:T(8,128)(2,1)}) custom-call(s32[2]{0:T(128)} %len_ref.1, s32[24]{0:T(128)} %cand_ref.1, bf16[32,1024]{1,0:T(8,128)(2,1)} %bitcast.6, bf16[64,1024]{1,0:T(8,128)(2,1)} %bitcast.5, bf16[4096]{0:T(1024)(128)(2,1)} %gain_ref.1, f32[2,96,128]{2,1,0:T(8,128)} %constant.2.clone.table_ref, ...), custom_call_target="tpu_custom_call" | custom-call | tf_op jit(solution)/shard_map/pallas_call | solution.py:415
  84.0 1.4 %copy.11 = bf16[2,16,512]{2,1,0:T(8,128)(2,1)} copy(bf16[2,16,512]{2,1,0:T(8,128)(2,1)} %bitcast.7) | data formatting | bytes 65536
  85.4 2.1 %copy.12 = bf16[24,32,512]{2,1,0:T(8,128)(2,1)} copy(bf16[24,32,512]{2,1,0:T(8,128)(2,1)} %bitcast.4) | data formatting | bytes 1572864
